TPU v7x, 1024 devices: a whole 4x4x32 slice. The times are simulated.
1024 devices in a mesh: dp: 4 (over z_hi), expert: 64 (over z_lo, x, core), mp: 4 (over y).
Axes of the slice: x: 4, y: 4, z: 32 (z_hi: 4, z_lo: 8; z = z_hi * 8 + z_lo), core: 2. Of those that a mesh axis runs over, the one named last changes fastest.
Arguments:
- x_rows: bfloat16 [32768, 3072], P(('dp', 'expert')), may hold values from -6 to 6, as said below
- dy_rows: bfloat16 [32768, 3072], P(('dp', 'expert')), may hold values from -1.5 to 1.5, as said below
- w_in: bfloat16 [64, 3072, 2, 1344], P('expert', None, None, 'mp'), may hold values from -0.109375 to 0.109375
- w_out: bfloat16 [64, 3072, 1344], P('expert', None, 'mp'), may hold values from -0.078125 to 0.078125
- counts: int32 [256, 64], P(('dp', 'expert')), may hold values from 0 to 2, as said below
- assign: int32 [1024, 4], P(('dp', 'expert')), may hold values from 0 to 15, as said below
Outputs:
- grad_w_in: bfloat16 [64, 3072, 2, 1344], P('expert', 'dp', None, 'mp')
- grad_w_out: bfloat16 [64, 3072, 1344], P('expert', 'dp', 'mp')
- grad_tokens: bfloat16 [1024, 3072], P(('dp', 'expert'), 'mp')
Inputs may be any that keep to these rules, and one draw needn't show every extreme that they name: counts[(g, u), s] is the number of tokens of owner s of group g that name expert e = u // 4 in assign, equal for the slices of one expert; it is at most 2, and 2 is reached in every group. `assign`: each token names 4 different experts; no owner names one expert for more than 2 of its tokens. `x_rows`: the 4 slices of one expert in one group keep equal copies of the same rows. `dy_rows`: the 4 slices of one expert in one group keep equal copies of the same rows.
All inputs are finite; a program needn't handle non-finite values.
Results may differ from a plain program's by a relative error of at most 0.018.
Values may be sent and summed in bfloat16 or wider, within the bound.
A program may use at most 64 MiB of HBM per device.

v0:
```python
import jax
import jax.numpy as jnp
from jax import lax
from jax.sharding import PartitionSpec as P

LAYER_EXPERTS = 16


def block_grads(x_block, dy_block, w_flat, w_down, live_mask):
    hidden_units = w_down.shape[1]
    preact = jnp.dot(x_block, w_flat, preferred_element_type=jnp.float32)
    gate_pre = preact[:, :hidden_units]
    up_pre = preact[:, hidden_units:]
    sigmoid_gate = jax.nn.sigmoid(gate_pre)
    hidden = (live_mask * gate_pre * sigmoid_gate * up_pre).astype(jnp.bfloat16)
    grad_hidden = jnp.dot(dy_block, w_down, preferred_element_type=jnp.float32)
    grad_gate = (
        live_mask * grad_hidden * up_pre * sigmoid_gate * (1.0 + gate_pre * (1.0 - sigmoid_gate))
    )
    grad_up = live_mask * grad_hidden * gate_pre * sigmoid_gate
    grad_pre = jnp.concatenate([grad_gate, grad_up], axis=1).astype(jnp.bfloat16)
    dx_partial = lax.dot_general(
        grad_pre, w_flat, (((1,), (1,)), ((), ())), preferred_element_type=jnp.float32
    )
    return (jnp.concatenate([grad_pre, hidden], axis=1), dx_partial)


def per_device(x_rows, dy_rows, w_in, w_out, counts, assign):
    slot_total, model_width = x_rows.shape
    hidden_units = w_out.shape[2]
    w_flat = w_in[0].reshape(model_width, 2 * hidden_units)
    w_down = w_out[0]
    per_source = counts[0]
    live_rows = jnp.sum(per_source)
    slot_index = jnp.arange(slot_total, dtype=jnp.int32)
    live_mask = (slot_index < live_rows).astype(jnp.float32)[:, None]
    block_acts, block_partial = block_grads(x_rows, dy_rows, w_flat, w_down, live_mask)
    summed_rows = lax.psum_scatter(
        block_partial.astype(jnp.bfloat16), "mp", scatter_dimension=1, tiled=True
    )
    owners = per_source.shape[0]
    capacity = slot_total // owners
    offsets = jnp.cumsum(per_source) - per_source
    lane_index = jnp.arange(capacity, dtype=jnp.int32)
    wanted = jnp.clip(offsets[:, None] + lane_index[None, :], 0, slot_total - 1).reshape(-1)
    present = lane_index[None, :] < per_source[:, None]
    source_rows = jnp.take(summed_rows, wanted, axis=0).reshape(owners, capacity, -1)
    outgoing = jnp.where(present[:, :, None], source_rows, jnp.zeros((), jnp.bfloat16))
    incoming = lax.all_to_all(outgoing, "expert", split_axis=0, concat_axis=0, tiled=True)
    units = lax.axis_size("expert")
    slices = units // min(LAYER_EXPERTS, units)
    tokens, route_width = assign.shape
    flat_routes = assign.reshape(-1)
    route_count = flat_routes.shape[0]
    token_of = jnp.arange(route_count, dtype=jnp.int32) // route_width
    same_expert = flat_routes[:, None] == flat_routes[None, :]
    earlier = token_of[None, :] < token_of[:, None]
    route_rank = jnp.sum((same_expert & earlier).astype(jnp.int32), axis=1)
    columns = jnp.arange(units * capacity, dtype=jnp.int32)
    column_expert = columns // capacity // slices
    column_rank = columns % capacity
    hits = (column_expert[None, :] == flat_routes[:, None]) & (
        column_rank[None, :] == route_rank[:, None]
    )
    selector = jnp.sum(hits.astype(jnp.float32).reshape(tokens, route_width, -1), axis=1).astype(
        jnp.bfloat16
    )
    grad_tokens = jnp.dot(
        selector, incoming.reshape(units * capacity, -1), preferred_element_type=jnp.float32
    ).astype(jnp.bfloat16)
    quarter = model_width // lax.axis_size("dp")
    act_column = jnp.arange(3 * hidden_units, dtype=jnp.int32)[None, :]
    zero_value = jnp.zeros((), jnp.bfloat16)
    stacked_acts = jnp.concatenate(
        [
            jnp.where(act_column < 2 * hidden_units, block_acts, zero_value),
            jnp.where(act_column >= 2 * hidden_units, block_acts, zero_value),
        ],
        axis=0,
    )
    stacked_cols = jnp.concatenate([x_rows, dy_rows], axis=0)
    summed_terms = lax.psum_scatter(
        lax.dot_general(
            stacked_cols, stacked_acts, (((0,), (0,)), ((), ())), preferred_element_type=jnp.float32
        ).astype(jnp.bfloat16),
        "dp",
        scatter_dimension=0,
        tiled=True,
    ).astype(jnp.float32)
    grad_w_in = (
        summed_terms[:, : 2 * hidden_units]
        .astype(jnp.bfloat16)
        .reshape(1, quarter, 2, hidden_units)
    )
    grad_w_out = (
        summed_terms[:, 2 * hidden_units :].astype(jnp.bfloat16).reshape(1, quarter, hidden_units)
    )
    return (grad_w_in, grad_w_out, grad_tokens)


def solution(mesh):
    return jax.shard_map(
        per_device,
        mesh=mesh,
        in_specs=(
            P(("dp", "expert"), None),
            P(("dp", "expert"), None),
            P("expert", None, None, "mp"),
            P("expert", None, "mp"),
            P(("dp", "expert"), None),
            P(("dp", "expert"), None),
        ),
        out_specs=(
            P("expert", "dp", None, "mp"),
            P("expert", "dp", "mp"),
            P(("dp", "expert"), "mp"),
        ),
        check_vma=False,
    )
```

profile of v0, /device:TPU:1, one launch (start us, length us, event | category | flops | bytes accessed | tf_op | source)
XLA Modules:
  0.0 516.7 jit_solution(18356149734995447256)
XLA Ops:
  7.2 1.4 reduce_sum.27
  8.7 0.6 compare_convert_fusion
  9.3 3.8 fusion.18
  13.2 0.7 multiply_convert_fusion.2
  13.9 1.7 convolution_convert_fusion.1
  15.7 0.3 broadcast_select_fusion.3
  16.0 5.5 %convolution_convert_fusion = bf16[3072,1008]{0,1:T(8,128)(2,1)} fusion(bf16[128,3072]{1,0:T(8,128)(2,1)} %param.7, bf16[128,3072]{1,0:T(8,128)(2,1)S(1)} %copy-done.2, bf16[128,1008]{0,1:T(8,128)(2,1)S(1)} %get-tuple-element.7, bf16[128,1008]{0,1:T(8,128)(2,1)S(1)} %get-tuple-element.6), kind=kOutput, calls=%fused_computation.1 | convolution fusion | flops 1592721408 | bytes 8282112 | tf_op jit(solution)/shard_map/dot_general | solution.py:83
  21.6 0.6 copy-done.5
  22.2 0.1 copy.11
  22.3 0.1 reduce-window.8
  22.4 0.1 reduce.1
  22.6 0.1 min.12
  22.8 0.1 iota_compare_fusion
  22.9 40.5 %reduce-scatter.5.cloned.1.call-done = bf16[128,768]{1,0:T(8,128)(2,1)} async-done(((bf16[128,3072]{1,0:T(8,128)(2,1)}), bf16[128,768]{1,0:T(8,128)(2,1)}) %reduce-scatter.5.cloned.1.call-update) | async-done | bytes 196624 | tf_op jit(solution)/shard_map/reduce_scatter | solution.py:38
  63.4 1.9 gather_fusion
  65.4 1.1 broadcast_select_fusion.1
  66.5 14.7 %all-to-all-start = ((bf16[64,2,768]{2,1,0:T(2,128)(2,1)}), bf16[64,2,768]{2,1,0:T(2,128)(2,1)S(1)}, u32[]{:S(2)}, u32[]{:S(2)}) async-start(bf16[64,2,768]{2,1,0:T(2,128)(2,1)} %broadcast_select_fusion.1), calls=%async_computation.2 | async-start | bytes 393216 | tf_op jit(solution)/shard_map/all_to_all | solution.py:49
  81.2 0.2 convert_reduce_fusion.1
  81.5 0.1 convert_reduce_fusion
  81.6 16.8 %all-to-all-done = bf16[64,2,768]{2,1,0:T(2,128)(2,1)S(1)} async-done(((bf16[64,2,768]{2,1,0:T(2,128)(2,1)}), bf16[64,2,768]{2,1,0:T(2,128)(2,1)S(1)}, u32[]{:S(2)}, u32[]{:S(2)}) %all-to-all-start) | async-done | bytes 196640 | tf_op jit(solution)/shard_map/all_to_all | solution.py:49
  98.5 0.7 convolution_convert_fusion.2
  99.3 406.5 %reduce-scatter.3.cloned.1.call-done = bf16[768,1008]{0,1:T(8,128)(2,1)} async-done(((bf16[3072,1008]{0,1:T(8,128)(2,1)}), bf16[768,1008]{0,1:T(8,128)(2,1)}) %reduce-scatter.3.cloned.1.call-update) | async-done | bytes 1548304 | tf_op jit(solution)/shard_map/reduce_scatter | solution.py:82
  505.8 1.9 slice_bitcast_fusion
  507.6 2.2 slice.22
  (26 shorter events, 0.6 us)
Async XLA Ops:
  7.2 6.0 %copy-start = (bf16[1,3072,336]{1,2,0:T(8,128)(2,1)S(1)}, bf16[1,3072,336]{1,2,0:T(8,128)(2,1)}, u32[]{:S(2)}) copy-start(bf16[1,3072,336]{1,2,0:T(8,128)(2,1)} %param.9) | copy-start | bytes 6193156
  7.2 6.0 %copy-start.3 = (bf16[128,3072]{1,0:T(8,128)(2,1)S(1)}, bf16[128,3072]{1,0:T(8,128)(2,1)}, u32[]{:S(2)}) copy-start(bf16[128,3072]{1,0:T(8,128)(2,1)} %param.7) | copy-start | bytes 2359300
  7.2 56.2 %reduce-scatter.5.cloned.1.call-start = ((), (), s32[]{:S(2)}) async-start(), calls=%async_computation.4 | async-start | bytes 983040 | tf_op jit(solution)/shard_map/reduce_scatter | solution.py:38
  9.3 4.5 copy-start.1
  13.9 2.1 copy-start.2
  15.6 490.2 %reduce-scatter.3.cloned.1.call-start = ((), (), s32[]{:S(2)}) async-start(), calls=%async_computation.3 | async-start | bytes 7741440 | tf_op jit(solution)/shard_map/reduce_scatter | solution.py:82
  21.6 0.7 copy-start.5
  21.6 59.5 %copy-start.4 = (s32[4,4]{1,0:T(4,128)S(1)}, s32[4,4]{1,0:T(4,128)}, u32[]{:S(2)}) copy-start(s32[4,4]{1,0:T(4,128)} %param.11) | copy-start | bytes 196
  66.5 32.0 %all-to-all-start = ((bf16[64,2,768]{2,1,0:T(2,128)(2,1)}), bf16[64,2,768]{2,1,0:T(2,128)(2,1)S(1)}, u32[]{:S(2)}, u32[]{:S(2)}) async-start(bf16[64,2,768]{2,1,0:T(2,128)(2,1)} %broadcast_select_fusion.1), calls=%async_computation.2 | async-start | bytes 393216 | tf_op jit(solution)/shard_map/all_to_all | solution.py:49
Sparse Core Ops, SparseCore 0:
  15.7 47.6 reduce-scatter.4
  66.8 438.8 reduce-scatter.2
where the time goes:
time: 526 us; the launch traced here: 517 us
  waiting for transfers between devices  464 us (88%)
  starting transfers between devices  14.7 us (3%)
  between operations  14.2 us (3%)
  matrix products  12.5 us (2%)
  local copies, waits for them, and re-layouts  7.22 us (1%)
    reduce_scatter x1, waiting for transfers between devices, per_device(): lax.psum_scatter(lax.dot_general(stacked_cols, stacked_acts, (((0,), (0,)...  407 us
    reduce_scatter x1, waiting for transfers between devices, per_device(): lax.psum_scatter(block_partial.astype(jnp.bfloat16), 'mp', scatter_dimens...  40.5 us
    all_to_all x1, waiting for transfers between devices, per_device(): lax.all_to_all(outgoing, 'expert', split_axis=0, concat_axis=0, tiled=True)  16.8 us
    all_to_all x1, starting transfers between devices, per_device(): lax.all_to_all(outgoing, 'expert', split_axis=0, concat_axis=0, tiled=True)  14.7 us
  transfers between devices with their start and end apart: 3, of which 3 were waited for; matrix products, arithmetic and copies ran while one was open for 2% of the time, Pallas kernels for 0%

commit v1 on v0

v1 whole, which is shorter than its diff:
```python
import jax
import jax.numpy as jnp
from jax import lax
from jax.experimental import pallas as pl
from jax.experimental.pallas import tpu as pltpu
from jax.sharding import PartitionSpec as P

MESH = pl.DeviceIdType.MESH
N_DP = 4
N_MP = 4
SLICES = 4
EXPERTS = 16
SLOTS = 128
QUARTERS = 4

ROUNDS = (
    ((3, 0), (1, 3)),
    ((3, 1), (1, 2)),
    ((3, 2), (1, 1)),
    ((3, 3), (1, 0)),
    ((2, 0), (2, 3)),
    ((2, 1), (2, 2)),
)
CHUNKS = tuple(chunk for pair in ROUNDS for chunk in pair)


def fused_kernel(
    x_ref, dy_ref, w_ref, wo_ref, counts_ref, assign_ref,
    gin_ref, gout_ref, gtok_ref,
    rows, w_in, w_out, acc, gpt, hdt, parts, got_f, sums, got_y, sent_t, got_t, comb,
    load_sem, zs, zr, xs, xr, ys, yr, cs, cr, fs, fr, ms, mr, ts, tr,
):
    units = w_out.shape[0]
    model = w_in.shape[1]
    quarter = model // QUARTERS
    g = lax.axis_index("dp")
    u = lax.axis_index("expert")
    m = lax.axis_index("mp")
    core = lax.rem(u, 2)
    half_x = lax.rem(lax.div(u, 2), 2)
    f = lax.rem(u, SLICES)
    e = lax.div(u, SLICES)
    plane_f = lax.div(lax.div(u, 8), 2)
    flip_core = 1 - 2 * core
    flip_x = 2 - 4 * half_x
    f_shift = (flip_core, flip_x, flip_core + flip_x)
    left_g, right_g = lax.rem(g + N_DP - 1, N_DP), lax.rem(g + 1, N_DP)
    m_at = [lax.rem(m + step, N_MP) for step in range(N_MP)]

    def loads():
        out = []
        for q in range(QUARTERS):
            cols = pl.ds(q * quarter, quarter)
            out.append(pltpu.make_async_copy(dy_ref.at[:, cols], rows.at[1, 0, q], load_sem.at[q]))
            out.append(pltpu.make_async_copy(x_ref.at[:, cols], rows.at[0, 0, q], load_sem.at[4 + q]))
        out.append(pltpu.make_async_copy(w_ref, w_in, load_sem.at[8]))
        out.append(pltpu.make_async_copy(wo_ref, w_out, load_sem.at[9]))
        return out

    local = loads()
    for copy in local:
        copy.start()

    barrier = pltpu.get_barrier_semaphore()

    def hello(where):
        pl.semaphore_signal(barrier, inc=1, device_id=where, device_id_type=MESH)

    hello({"dp": left_g})
    hello({"dp": right_g})
    for shift in f_shift:
        hello({"expert": u + shift})
    for step in range(1, N_MP):
        hello({"mp": m_at[step]})
    for expert in range(EXPERTS):
        source = expert * SLICES + plane_f

        @pl.when(source != u)
        def _():
            hello({"expert": source})

    own_target = (plane_f == f).astype(jnp.int32)

    counts = counts_ref[...].astype(jnp.float32)
    live_rows = jnp.sum(counts, axis=1, keepdims=True)
    row_at = lax.broadcasted_iota(jnp.int32, (SLOTS, 1), 0)
    live = row_at.astype(jnp.float32) < live_rows
    for q in range(QUARTERS):
        local[2 * q].wait()
        dy = rows[1, 0, q]
        rows[1, 0, q] = jnp.where(live, dy, jnp.zeros_like(dy))
        local[2 * q + 1].wait()

    pl.semaphore_wait(barrier, 8 + EXPERTS - own_target)

    def rcopy(src, dst, send, recv, where):
        return pltpu.make_async_remote_copy(
            src_ref=src, dst_ref=dst, send_sem=send, recv_sem=recv, device_id=where, device_id_type=MESH
        )

    def at(kind, distance, q, start, size):
        return rows.at[kind, distance, q, pl.ds(pl.multiple_of(start, 16), size)]

    own_16 = m * 32 + half_x * 16
    pair_16 = m * 32 + (1 - half_x) * 16

    def z_copy(i):
        distance, q = CHUNKS[i]
        dst = at(core, distance, q, own_16, 16)
        if distance == 3:
            return rcopy(at(core, 0, q, own_16, 16), dst, zs.at[i], zr.at[i], {"dp": right_g})
        if distance == 1:
            return rcopy(at(core, 0, q, own_16, 16), dst, zs.at[i], zr.at[i], {"dp": left_g})
        if q < 2:
            return rcopy(at(core, 3, q, own_16, 16), dst, zs.at[i], zr.at[i], {"dp": right_g})
        return rcopy(at(core, 1, q, own_16, 16), dst, zs.at[i], zr.at[i], {"dp": left_g})

    def x_copy(i, start):
        d, q = CHUNKS[i]
        block = at(core, d, q, start, 16)
        return rcopy(block, block, xs.at[i], xr.at[i], {"expert": u + flip_x})

    def y_copy(i, way, block_m):
        d, q = CHUNKS[i]
        block = at(core, d, q, block_m * 32, 32)
        j = 4 * i + way
        return rcopy(block, block, ys.at[j], yr.at[j], {"mp": m_at[1] if way == 0 else m_at[3]})

    def y_forward(i, way, block_m):
        d, q = CHUNKS[i]
        block = at(core, d, q, block_m * 32 + 16 * way, 16)
        j = 4 * i + 2 + way
        return rcopy(block, block, ys.at[j], yr.at[j], {"mp": m_at[1] if way == 0 else m_at[3]})

    def c_copy(i, kind):
        d, q = CHUNKS[i]
        block = rows.at[kind, d, q]
        return rcopy(block, block, cs.at[i], cr.at[i], {"expert": u + flip_core})

    for i in range(8):
        z_copy(i).start()

    def stage_z(k):
        for i in (2 * k, 2 * k + 1):
            z_copy(i).wait_recv()
            if k < 2:
                z_copy(8 + i).start()
            x_copy(i, own_16).start()

    def stage_x(k):
        for i in (2 * k, 2 * k + 1):
            x_copy(i, pair_16).wait_recv()
            for way in range(2):
                y_copy(i, way, m).start()

    def stage_y(k):
        for i in (2 * k, 2 * k + 1):
            y_copy(i, 0, m_at[3]).wait_recv()
            y_forward(i, 0, m_at[3]).start()
            y_copy(i, 1, m_at[1]).wait_recv()
            y_forward(i, 1, m_at[1]).start()

    def stage_f(k):
        for i in (2 * k, 2 * k + 1):
            for way in range(2):
                y_forward(i, way, m_at[2]).wait_recv()
            c_copy(i, core).start()

    def multiply(d, q):
        cols = pl.ds(q * quarter, quarter)
        pre = lax.dot_general(
            w_in[:, cols], rows[0, d, q], (((1,), (1,)), ((), ())), preferred_element_type=jnp.float32
        )
        grad = lax.dot_general(
            w_out[:, cols], rows[1, d, q], (((1,), (1,)), ((), ())), preferred_element_type=jnp.float32
        )
        return pre, grad

    def stage_c(k):
        for i in (2 * k, 2 * k + 1):
            c_copy(i, 1 - core).wait_recv()
            d, q = CHUNKS[i]
            pre, grad = multiply(d, q)
            first = i < 2 or i == 8
            if first:
                acc[d, : 2 * units] = pre
                acc[d, 2 * units :] = grad
            else:
                acc[d, : 2 * units] += pre
                acc[d, 2 * units :] += grad

    def activate(d):
        gate = acc[d, :units]
        up = acc[d, units : 2 * units]
        grad = acc[d, 2 * units :]
        sigmoid = jax.nn.sigmoid(gate)
        lanes = pl.ds(d * SLOTS, SLOTS)
        hdt[:, lanes] = (gate * sigmoid * up).astype(jnp.bfloat16)
        gpt[:units, lanes] = (grad * up * sigmoid * (1.0 + gate * (1.0 - sigmoid))).astype(jnp.bfloat16)
        gpt[units:, lanes] = (grad * gate * sigmoid).astype(jnp.bfloat16)

    local[8].wait()
    local[9].wait()
    for q in range(QUARTERS):
        pre, grad = multiply(0, q)
        if q == 0:
            acc[0, : 2 * units] = pre
            acc[0, 2 * units :] = grad
        else:
            acc[0, : 2 * units] += pre
            acc[0, 2 * units :] += grad
    activate(0)

    place = lax.broadcasted_iota(jnp.int32, (SLOTS, 1), 0)
    owner = jnp.right_shift(lax.broadcasted_iota(jnp.int32, (SLOTS, 64), 0), 1)
    other = lax.broadcasted_iota(jnp.int32, (SLOTS, 64), 1)
    spread = jnp.broadcast_to(counts, (SLOTS, 64))
    zero = jnp.zeros_like(spread)
    start = jnp.sum(jnp.where(other < owner, spread, zero), axis=1, keepdims=True)
    held = jnp.sum(jnp.where(other == owner, spread, zero), axis=1, keepdims=True)
    rank = jnp.bitwise_and(place, 1).astype(jnp.float32)
    wanted = jnp.where(rank < held, start + rank, -1.0)
    slot_at = lax.broadcasted_iota(jnp.int32, (SLOTS, SLOTS), 1).astype(jnp.float32)
    order = jnp.where(slot_at == wanted, 1.0, 0.0).astype(jnp.bfloat16)
    ordered = lax.dot_general(
        order, gpt[:, :SLOTS], (((1,), (1,)), ((), ())), preferred_element_type=jnp.float32
    ).astype(jnp.bfloat16)
    for q in range(QUARTERS):
        cols = pl.ds(q * quarter, quarter)
        parts[:, cols] = jnp.dot(ordered, w_in[:, cols], preferred_element_type=jnp.float32).astype(
            jnp.bfloat16
        )

    def f_copy(j):
        target = f + f_shift[j]
        src = parts.at[pl.ds(pl.multiple_of(target * 32, 32), 32)]
        return rcopy(src, got_f.at[j], fs.at[j], fr.at[j], {"expert": u + f_shift[j]})

    for j in range(3):
        f_copy(j).start()

    def sum_slices():
        for j in range(3):
            f_copy(j).wait_recv()
        mine = pl.ds(pl.multiple_of(f * 32, 32), 32)
        for q in range(QUARTERS):
            cols = pl.ds(q * quarter, quarter)
            total = parts[mine, cols].astype(jnp.float32)
            for j in range(3):
                total = total + got_f[j, :, cols].astype(jnp.float32)
            sums[q] = total.astype(jnp.bfloat16)
        for step in range(1, N_MP):
            m_copy(step).start()

    def m_copy(step):
        return rcopy(
            sums.at[m_at[step]], got_y.at[step - 1], ms.at[step - 1], mr.at[step - 1], {"mp": m_at[step]}
        )

    def token_copy(i):
        return rcopy(sent_t.at[i], got_t.at[e], ts.at[i], tr.at[e], {"expert": 16 * f + i})

    def token_arrival(expert):
        return rcopy(
            sent_t.at[expert], got_t.at[expert], ts.at[expert], tr.at[expert], {"expert": u}
        )

    def token_local(i):
        return pltpu.make_async_copy(sent_t.at[i], got_t.at[e], tr.at[e])

    def sum_mp():
        total = sums[m].astype(jnp.float32)
        for step in range(1, N_MP):
            m_copy(step).wait_recv()
            total = total + got_y[step - 1].astype(jnp.float32)
        for i in range(16):
            sent_t[i] = total[2 * i : 2 * i + 2].astype(jnp.bfloat16)
        for i in range(16):

            @pl.when(16 * f + i != u)
            def _():
                token_copy(i).start()

            @pl.when(16 * f + i == u)
            def _():
                token_local(i).start()

    def combine():
        for expert in range(EXPERTS):
            source = expert * SLICES + plane_f

            @pl.when(source != u)
            def _():
                token_arrival(expert).wait_recv()

            @pl.when(source == u)
            def _():
                pltpu.make_async_copy(sent_t.at[expert], got_t.at[expert], tr.at[expert]).wait()

            comb[pl.ds(2 * expert, 2)] = got_t[expert].astype(jnp.float32)
        column = lax.broadcasted_iota(jnp.int32, (8, 2 * EXPERTS), 1)
        token = lax.broadcasted_iota(jnp.int32, (8, 2 * EXPERTS), 0)
        expert_at = jnp.right_shift(column, 1)
        rank_at = jnp.bitwise_and(column, 1)
        seen = jnp.zeros_like(column)
        pick = jnp.zeros((8, 2 * EXPERTS), jnp.float32)
        for t in range(assign_ref.shape[0]):
            named = jnp.zeros_like(column)
            for k in range(assign_ref.shape[1]):
                named = named + jnp.where(expert_at == assign_ref[t, k], 1, 0)
            hit = jnp.where(seen == rank_at, named, 0)
            pick = jnp.where(token == t, hit.astype(jnp.float32), pick)
            seen = seen + named
        out = jnp.dot(
            pick.astype(jnp.bfloat16), comb[...].astype(jnp.bfloat16), preferred_element_type=jnp.float32
        )
        gtok_ref[...] = out[: gtok_ref.shape[0]].astype(jnp.bfloat16)

    stage_z(0)
    stage_x(0)
    stage_z(1)
    stage_y(0)
    sum_slices()
    stage_x(1)
    stage_f(0)
    stage_z(2)
    stage_c(0)
    stage_y(1)
    stage_x(2)
    sum_mp()
    stage_f(1)
    stage_z(3)
    stage_c(1)
    stage_y(2)
    stage_x(3)
    stage_f(2)
    stage_z(4)
    stage_c(2)
    stage_y(3)
    stage_x(4)
    stage_f(3)
    stage_z(5)
    stage_y(4)
    stage_x(5)
    stage_c(3)
    stage_f(4)
    combine()
    activate(1)
    activate(3)
    stage_y(5)
    stage_c(4)
    stage_f(5)
    stage_c(5)
    activate(2)

    x_all = rows[0, :, g].reshape(N_DP * SLOTS, quarter)
    gin_ref[...] = jnp.dot(gpt[...], x_all, preferred_element_type=jnp.float32).astype(jnp.bfloat16)
    dy_all = rows[1, :, g].reshape(N_DP * SLOTS, quarter)
    gout_ref[...] = jnp.dot(hdt[...], dy_all, preferred_element_type=jnp.float32).astype(jnp.bfloat16)

    for i in range(12):
        z_copy(i).wait_send()
        x_copy(i, own_16).wait_send()
        for way in range(2):
            y_copy(i, way, m).wait_send()
            y_forward(i, way, m_at[3] if way == 0 else m_at[1]).wait_send()
        c_copy(i, core).wait_send()
    for j in range(3):
        f_copy(j).wait_send()
        m_copy(j + 1).wait_send()
    for i in range(16):

        @pl.when(16 * f + i != u)
        def _():
            token_copy(i).wait_send()


def per_device(x_rows, dy_rows, w_in, w_out, counts, assign):
    model = w_in.shape[1]
    units = w_in.shape[3]
    quarter = model // QUARTERS
    w_flat = jnp.transpose(w_in[0], (1, 2, 0)).reshape(2 * units, model)
    w_down = jnp.transpose(w_out[0], (1, 0))
    bf16, f32 = jnp.bfloat16, jnp.float32
    dma = pltpu.SemaphoreType.DMA
    anywhere = pl.BlockSpec(memory_space=pl.ANY)
    vmem = pl.BlockSpec(memory_space=pltpu.VMEM)
    smem = pl.BlockSpec(memory_space=pltpu.SMEM)
    grad_in, grad_out, grad_tokens = pl.pallas_call(
        fused_kernel,
        out_shape=(
            jax.ShapeDtypeStruct((2 * units, quarter), bf16),
            jax.ShapeDtypeStruct((units, quarter), bf16),
            jax.ShapeDtypeStruct((assign.shape[0], quarter), bf16),
        ),
        in_specs=[anywhere, anywhere, anywhere, anywhere, vmem, smem],
        out_specs=(vmem, vmem, vmem),
        scratch_shapes=[
            pltpu.VMEM((2, N_DP, QUARTERS, SLOTS, quarter), bf16),
            pltpu.VMEM((2 * units, model), bf16),
            pltpu.VMEM((units, model), bf16),
            pltpu.VMEM((N_DP, 3 * units, SLOTS), f32),
            pltpu.VMEM((2 * units, N_DP * SLOTS), bf16),
            pltpu.VMEM((units, N_DP * SLOTS), bf16),
            pltpu.VMEM((SLOTS, model), bf16),
            pltpu.VMEM((3, 32, model), bf16),
            pltpu.VMEM((N_MP, 32, quarter), bf16),
            pltpu.VMEM((3, 32, quarter), bf16),
            pltpu.VMEM((16, 2, quarter), bf16),
            pltpu.VMEM((EXPERTS, 2, quarter), bf16),
            pltpu.VMEM((2 * EXPERTS, quarter), f32),
            dma((10,)),
            dma((12,)), dma((12,)),
            dma((12,)), dma((12,)),
            dma((48,)), dma((48,)),
            dma((12,)), dma((12,)),
            dma((3,)), dma((3,)),
            dma((3,)), dma((3,)),
            dma((16,)), dma((EXPERTS,)),
        ],
        compiler_params=pltpu.CompilerParams(
            collective_id=0, has_side_effects=True, vmem_limit_bytes=48 * 1024 * 1024
        ),
        cost_estimate=pl.CostEstimate(flops=5 * 10**9, bytes_accessed=10**7, transcendentals=10**6),
    )(x_rows, dy_rows, w_flat, w_down, counts, assign)
    grad_w_in = jnp.transpose(grad_in.reshape(2, units, quarter), (2, 0, 1))[None]
    grad_w_out = jnp.transpose(grad_out, (1, 0))[None]
    return grad_w_in, grad_w_out, grad_tokens


def solution(mesh):
    return jax.shard_map(
        per_device,
        mesh=mesh,
        in_specs=(
            P(("dp", "expert"), None),
            P(("dp", "expert"), None),
            P("expert", None, None, "mp"),
            P("expert", None, "mp"),
            P(("dp", "expert"), None),
            P(("dp", "expert"), None),
        ),
        out_specs=(
            P("expert", "dp", None, "mp"),
            P("expert", "dp", "mp"),
            P(("dp", "expert"), "mp"),
        ),
        check_vma=False,
    )
```

time: 526 us -> 100 us (0.19); the launches traced: 517 us -> 99.9 us
  waiting for transfers between devices: 464 us -> 0 us
  Pallas kernels: 0 us -> 91.7 us
  starting transfers between devices: 14.7 us -> 0 us
  between operations: 14.2 us -> 0.65 us
  matrix products: 12.5 us -> 0 us
    reduce_scatter x2 -> x0, waiting for transfers between devices: 447 us -> none  [the longest x1 407 us: per_device(): lax.psum_scatter(lax.dot_general(stacked_cols, stacked_acts, (((0,), (0,)...]
    pallas_call x0 -> x1, Pallas kernels: none -> 91.7 us  [per_device(): pl.pallas_call(fused_kernel, out_shape=(jax.ShapeDtypeStruct((2 * units,...]
    all_to_all x1 -> x0, waiting for transfers between devices: 16.8 us -> none  [per_device(): lax.all_to_all(outgoing, 'expert', split_axis=0, concat_axis=0, tiled=True)]
    all_to_all x1 -> x0, starting transfers between devices: 14.7 us -> none  [per_device(): lax.all_to_all(outgoing, 'expert', split_axis=0, concat_axis=0, tiled=True)]
    dot_general x5 -> x0, matrix products: 12.5 us -> none  [the longest x1 5.53 us: per_device(): lax.dot_general(stacked_cols, stacked_acts, (((0,), (0,)), ((), ())), pre...]
    unnamed x12 -> x13, local copies, waits for them, and re-layouts: 0.65 us -> 7.52 us
  transfers between devices with their start and end apart: 3 -> 0, of which waited for: 3 -> 0; matrix products, arithmetic and copies ran while one was open for 2% -> 0% of each run, Pallas kernels for 0% -> 0%
where the time goes in v1:
time: 100 us; the launch traced here: 99.9 us
  Pallas kernels  91.7 us (92%)
  local copies, waits for them, and re-layouts  7.52 us (8%)
    pallas_call x1, Pallas kernels, per_device(): pl.pallas_call(fused_kernel, out_shape=(jax.ShapeDtypeStruct((2 * units,...  91.7 us
    unnamed x13, local copies, waits for them, and re-layouts  7.52 us

profile of v1, /device:TPU:1, one launch (start us, length us, event | category | flops | bytes accessed | tf_op | source)
XLA Modules:
  0.0 99.9 jit_solution(10935081509142131181)
XLA Ops:
  0.6 0.0 copy-start
  0.6 1.6 %copy-done = bf16[1,3072,336]{1,2,0:T(8,128)(2,1)S(1)} copy-done((bf16[1,3072,336]{1,2,0:T(8,128)(2,1)S(1)}, bf16[1,3072,336]{1,2,0:T(8,128)(2,1)}, u32[]{:S(2)}) %copy-start) | copy-done | bytes 2064408
  2.2 0.0 copy-start.1
  2.2 1.1 %copy-done.1 = bf16[128,3072]{1,0:T(8,128)(2,1)S(1)} copy-done((bf16[128,3072]{1,0:T(8,128)(2,1)S(1)}, bf16[128,3072]{1,0:T(8,128)(2,1)}, u32[]{:S(2)}) %copy-start.1) | copy-done | bytes 786456
  3.3 0.0 copy-start.2
  3.3 1.1 %copy-done.2 = bf16[128,3072]{1,0:T(8,128)(2,1)S(1)} copy-done((bf16[128,3072]{1,0:T(8,128)(2,1)S(1)}, bf16[128,3072]{1,0:T(8,128)(2,1)}, u32[]{:S(2)}) %copy-start.2) | copy-done | bytes 786456
  4.5 0.0 copy-start.3
  4.5 0.7 copy-done.3
  5.2 0.0 copy-start.4
  5.2 0.7 copy-done.4
  5.8 91.7 %shard_map.85 = (bf16[672,768]{1,0:T(8,128)(2,1)S(1)}, bf16[336,768]{1,0:T(8,128)(2,1)S(1)}, bf16[4,768]{1,0:T(4,128)(2,1)S(1)}) custom-call(bf16[128,3072]{1,0:T(8,128)(2,1)S(1)} %copy-done.1, bf16[128,3072]{1,0:T(8,128)(2,1)S(1)} %copy-done.2, bf16[672,3072]{1,0:T(8,128)(2,1)} %bitcast.19, bf16[336,3072]{1,0:T(8,128)(2,1)S(1)} %bitcast.18, ...), custom_call_target="tpu_custom_call" | custom-call | flops 5000000000 | bytes 10000000 | tf_op jit(solution)/shard_map/pallas_call | solution.py:389
  97.6 1.0 copy.12
  98.5 0.8 copy.13
  99.3 0.6 copy.14
Async XLA Ops:
  0.6 1.6 %copy-start = (bf16[1,3072,336]{1,2,0:T(8,128)(2,1)S(1)}, bf16[1,3072,336]{1,2,0:T(8,128)(2,1)}, u32[]{:S(2)}) copy-start(bf16[1,3072,336]{1,2,0:T(8,128)(2,1)} %param.9) | copy-start | bytes 6193156
  2.2 1.1 %copy-start.1 = (bf16[128,3072]{1,0:T(8,128)(2,1)S(1)}, bf16[128,3072]{1,0:T(8,128)(2,1)}, u32[]{:S(2)}) copy-start(bf16[128,3072]{1,0:T(8,128)(2,1)} %x_ref.1) | copy-start | bytes 2359300
  3.3 1.1 %copy-start.2 = (bf16[128,3072]{1,0:T(8,128)(2,1)S(1)}, bf16[128,3072]{1,0:T(8,128)(2,1)}, u32[]{:S(2)}) copy-start(bf16[128,3072]{1,0:T(8,128)(2,1)} %dy_ref.1) | copy-start | bytes 2359300
  4.5 0.7 copy-start.3
  5.2 0.7 copy-start.4

commit v2 on v1

--- a/solution.py
+++ b/solution.py
@@ -12,6 +12,7 @@
 EXPERTS = 16
 SLOTS = 128
 QUARTERS = 4
+VMEM_LIMIT = 56 * 1024 * 1024
 
 ROUNDS = (
     ((3, 0), (1, 3)),
@@ -21,13 +22,14 @@
     ((2, 0), (2, 3)),
     ((2, 1), (2, 2)),
 )
+WINDOW = 3
 CHUNKS = tuple(chunk for pair in ROUNDS for chunk in pair)
 
 
 def fused_kernel(
     x_ref, dy_ref, w_ref, wo_ref, counts_ref, assign_ref,
     gin_ref, gout_ref, gtok_ref,
-    rows, w_in, w_out, acc, gpt, hdt, parts, got_f, sums, got_y, sent_t, got_t, comb,
+    own, rows, w_in, w_out, acc, terms, gpt, hdt, parts, got_f, sums, got_y, sent_t, got_t, comb,
     load_sem, zs, zr, xs, xr, ys, yr, cs, cr, fs, fr, ms, mr, ts, tr,
 ):
     units = w_out.shape[0]
@@ -47,18 +49,22 @@
     left_g, right_g = lax.rem(g + N_DP - 1, N_DP), lax.rem(g + 1, N_DP)
     m_at = [lax.rem(m + step, N_MP) for step in range(N_MP)]
 
-    def loads():
-        out = []
-        for q in range(QUARTERS):
-            cols = pl.ds(q * quarter, quarter)
-            out.append(pltpu.make_async_copy(dy_ref.at[:, cols], rows.at[1, 0, q], load_sem.at[q]))
-            out.append(pltpu.make_async_copy(x_ref.at[:, cols], rows.at[0, 0, q], load_sem.at[4 + q]))
-        out.append(pltpu.make_async_copy(w_ref, w_in, load_sem.at[8]))
-        out.append(pltpu.make_async_copy(wo_ref, w_out, load_sem.at[9]))
-        return out
-
-    local = loads()
-    for copy in local:
+    own_16 = m * 32 + half_x * 16
+    pair_16 = m * 32 + (1 - half_x) * 16
+    share = pl.ds(pl.multiple_of(own_16, 16), 16)
+    early = []
+    for q in range(QUARTERS):
+        cols = pl.ds(q * quarter, quarter)
+        early.append(pltpu.make_async_copy(x_ref.at[share, cols], own.at[0, q], load_sem.at[10 + q]))
+        early.append(pltpu.make_async_copy(dy_ref.at[share, cols], own.at[1, q], load_sem.at[14 + q]))
+    local = []
+    for q in range(QUARTERS):
+        cols = pl.ds(q * quarter, quarter)
+        local.append(pltpu.make_async_copy(dy_ref.at[:, cols], rows.at[1, 0, q], load_sem.at[q]))
+        local.append(pltpu.make_async_copy(x_ref.at[:, cols], rows.at[0, 0, q], load_sem.at[4 + q]))
+    local.append(pltpu.make_async_copy(w_ref, w_in, load_sem.at[8]))
+    local.append(pltpu.make_async_copy(wo_ref, w_out, load_sem.at[9]))
+    for copy in early:
         copy.start()
 
     barrier = pltpu.get_barrier_semaphore()
@@ -85,11 +91,15 @@
     live_rows = jnp.sum(counts, axis=1, keepdims=True)
     row_at = lax.broadcasted_iota(jnp.int32, (SLOTS, 1), 0)
     live = row_at.astype(jnp.float32) < live_rows
-    for q in range(QUARTERS):
-        local[2 * q].wait()
-        dy = rows[1, 0, q]
-        rows[1, 0, q] = jnp.where(live, dy, jnp.zeros_like(dy))
-        local[2 * q + 1].wait()
+    for copy in early:
+        copy.wait()
+    for copy in local:
+        copy.start()
+    own_row = lax.broadcasted_iota(jnp.int32, (16, 1), 0) + own_16
+    own_live = own_row.astype(jnp.float32) < live_rows
+    for q in range(QUARTERS):
+        dy = own[1, q]
+        own[1, q] = jnp.where(own_live, dy, jnp.zeros_like(dy))
 
     pl.semaphore_wait(barrier, 8 + EXPERTS - own_target)
 
@@ -100,17 +110,14 @@
 
     def at(kind, distance, q, start, size):
         return rows.at[kind, distance, q, pl.ds(pl.multiple_of(start, 16), size)]
-
-    own_16 = m * 32 + half_x * 16
-    pair_16 = m * 32 + (1 - half_x) * 16
 
     def z_copy(i):
         distance, q = CHUNKS[i]
         dst = at(core, distance, q, own_16, 16)
         if distance == 3:
-            return rcopy(at(core, 0, q, own_16, 16), dst, zs.at[i], zr.at[i], {"dp": right_g})
+            return rcopy(own.at[core, q], dst, zs.at[i], zr.at[i], {"dp": right_g})
         if distance == 1:
-            return rcopy(at(core, 0, q, own_16, 16), dst, zs.at[i], zr.at[i], {"dp": left_g})
+            return rcopy(own.at[core, q], dst, zs.at[i], zr.at[i], {"dp": left_g})
         if q < 2:
             return rcopy(at(core, 3, q, own_16, 16), dst, zs.at[i], zr.at[i], {"dp": right_g})
         return rcopy(at(core, 1, q, own_16, 16), dst, zs.at[i], zr.at[i], {"dp": left_g})
@@ -137,14 +144,14 @@
         block = rows.at[kind, d, q]
         return rcopy(block, block, cs.at[i], cr.at[i], {"expert": u + flip_core})
 
-    for i in range(8):
+    for i in range(2 * WINDOW):
         z_copy(i).start()
 
     def stage_z(k):
         for i in (2 * k, 2 * k + 1):
             z_copy(i).wait_recv()
-            if k < 2:
-                z_copy(8 + i).start()
+            if k + WINDOW < len(ROUNDS):
+                z_copy(i + 2 * WINDOW).start()
             x_copy(i, own_16).start()
 
     def stage_x(k):
@@ -199,6 +206,11 @@
         gpt[:units, lanes] = (grad * up * sigmoid * (1.0 + gate * (1.0 - sigmoid))).astype(jnp.bfloat16)
         gpt[units:, lanes] = (grad * gate * sigmoid).astype(jnp.bfloat16)
 
+    for q in range(QUARTERS):
+        local[2 * q].wait()
+        dy = rows[1, 0, q]
+        rows[1, 0, q] = jnp.where(live, dy, jnp.zeros_like(dy))
+        local[2 * q + 1].wait()
     local[8].wait()
     local[9].wait()
     for q in range(QUARTERS):
@@ -316,63 +328,84 @@
         )
         gtok_ref[...] = out[: gtok_ref.shape[0]].astype(jnp.bfloat16)
 
-    stage_z(0)
-    stage_x(0)
-    stage_z(1)
-    stage_y(0)
-    sum_slices()
-    stage_x(1)
-    stage_f(0)
-    stage_z(2)
-    stage_c(0)
-    stage_y(1)
-    stage_x(2)
-    sum_mp()
-    stage_f(1)
-    stage_z(3)
-    stage_c(1)
-    stage_y(2)
-    stage_x(3)
-    stage_f(2)
-    stage_z(4)
-    stage_c(2)
-    stage_y(3)
-    stage_x(4)
-    stage_f(3)
-    stage_z(5)
-    stage_y(4)
-    stage_x(5)
-    stage_c(3)
-    stage_f(4)
-    combine()
-    activate(1)
-    activate(3)
-    stage_y(5)
-    stage_c(4)
-    stage_f(5)
-    stage_c(5)
+    def sum_terms(part):
+        two = pl.ds(2 * part, 2)
+        lanes = pl.ds(2 * part * SLOTS, 2 * SLOTS)
+        x_two = rows[0, two, g].reshape(2 * SLOTS, quarter)
+        dy_two = rows[1, two, g].reshape(2 * SLOTS, quarter)
+        g_in = jnp.dot(gpt[:, lanes], x_two, preferred_element_type=jnp.float32)
+        g_out = jnp.dot(hdt[:, lanes], dy_two, preferred_element_type=jnp.float32)
+        if part == 0:
+            terms[: 2 * units] = g_in
+            terms[2 * units :] = g_out
+        else:
+            gin_ref[...] = (terms[: 2 * units] + g_in).astype(jnp.bfloat16)
+            gout_ref[...] = (terms[2 * units :] + g_out).astype(jnp.bfloat16)
+
+    def sent(k):
+        for i in (2 * k, 2 * k + 1):
+            z_copy(i).wait_send()
+            x_copy(i, own_16).wait_send()
+            for way in range(2):
+                y_copy(i, way, m).wait_send()
+                y_forward(i, way, m_at[3] if way == 0 else m_at[1]).wait_send()
+            c_copy(i, core).wait_send()
+
+    def rows_sent():
+        for j in range(3):
+            f_copy(j).wait_send()
+            m_copy(j + 1).wait_send()
+        for i in range(16):
+
+            @pl.when(16 * f + i != u)
+            def _():
+                token_copy(i).wait_send()
+
+    last = len(ROUNDS)
+    for t in range(last + 4):
+        if t < last:
+            stage_z(t)
+        if 1 <= t <= last:
+            stage_x(t - 1)
+        if 2 <= t <= last + 1:
+            stage_y(t - 2)
+        if 3 <= t <= last + 2:
+            stage_f(t - 3)
+        if t == 1:
+            sum_slices()
+        if t == 3:
+            sum_mp()
+        if t == last - 1:
+            combine()
+        if t == last:
+            rows_sent()
+        if t >= 4:
+            stage_c(t - 4)
+        if t == last + 1:
+            activate(1)
+            activate(3)
+            sum_terms(0)
+        if t >= 5 and t - 5 < last - 2:
+            sent(t - 5)
     activate(2)
 
-    x_all = rows[0, :, g].reshape(N_DP * SLOTS, quarter)
-    gin_ref[...] = jnp.dot(gpt[...], x_all, preferred_element_type=jnp.float32).astype(jnp.bfloat16)
-    dy_all = rows[1, :, g].reshape(N_DP * SLOTS, quarter)
-    gout_ref[...] = jnp.dot(hdt[...], dy_all, preferred_element_type=jnp.float32).astype(jnp.bfloat16)
-
-    for i in range(12):
-        z_copy(i).wait_send()
-        x_copy(i, own_16).wait_send()
-        for way in range(2):
-            y_copy(i, way, m).wait_send()
-            y_forward(i, way, m_at[3] if way == 0 else m_at[1]).wait_send()
-        c_copy(i, core).wait_send()
-    for j in range(3):
-        f_copy(j).wait_send()
-        m_copy(j + 1).wait_send()
-    for i in range(16):
-
-        @pl.when(16 * f + i != u)
-        def _():
-            token_copy(i).wait_send()
+    sum_terms(1)
+
+    sent(last - 2)
+    sent(last - 1)
+
+
+def copy_kernel(a_in, b_in, c_in, a_out, b_out, c_out, a_held, b_held, c_held, in_sem, out_sem):
+    held = (a_held, b_held, c_held)
+    reads = [pltpu.make_async_copy(src, held[i], in_sem.at[i]) for i, src in enumerate((a_in, b_in, c_in))]
+    writes = [pltpu.make_async_copy(held[i], dst, out_sem.at[i]) for i, dst in enumerate((a_out, b_out, c_out))]
+    for copy in reads:
+        copy.start()
+    for read, write in zip(reads, writes):
+        read.wait()
+        write.start()
+    for copy in writes:
+        copy.wait()
 
 
 def per_device(x_rows, dy_rows, w_in, w_out, counts, assign):
@@ -383,10 +416,10 @@
     w_down = jnp.transpose(w_out[0], (1, 0))
     bf16, f32 = jnp.bfloat16, jnp.float32
     dma = pltpu.SemaphoreType.DMA
-    anywhere = pl.BlockSpec(memory_space=pl.ANY)
+    anywhere = pl.BlockSpec(memory_space=pltpu.HBM)
     vmem = pl.BlockSpec(memory_space=pltpu.VMEM)
     smem = pl.BlockSpec(memory_space=pltpu.SMEM)
-    grad_in, grad_out, grad_tokens = pl.pallas_call(
+    held = pl.pallas_call(
         fused_kernel,
         out_shape=(
             jax.ShapeDtypeStruct((2 * units, quarter), bf16),
@@ -396,10 +429,12 @@
         in_specs=[anywhere, anywhere, anywhere, anywhere, vmem, smem],
         out_specs=(vmem, vmem, vmem),
         scratch_shapes=[
+            pltpu.VMEM((2, QUARTERS, 16, quarter), bf16),
             pltpu.VMEM((2, N_DP, QUARTERS, SLOTS, quarter), bf16),
             pltpu.VMEM((2 * units, model), bf16),
             pltpu.VMEM((units, model), bf16),
             pltpu.VMEM((N_DP, 3 * units, SLOTS), f32),
+            pltpu.VMEM((3 * units, quarter), f32),
             pltpu.VMEM((2 * units, N_DP * SLOTS), bf16),
             pltpu.VMEM((units, N_DP * SLOTS), bf16),
             pltpu.VMEM((SLOTS, model), bf16),
@@ -409,20 +444,29 @@
             pltpu.VMEM((16, 2, quarter), bf16),
             pltpu.VMEM((EXPERTS, 2, quarter), bf16),
             pltpu.VMEM((2 * EXPERTS, quarter), f32),
-            dma((10,)),
+            dma((18,)),
             dma((12,)), dma((12,)),
             dma((12,)), dma((12,)),
             dma((48,)), dma((48,)),
-            dma((12,)), dma((12,)),
+            dma((48,)), dma((48,)),
             dma((3,)), dma((3,)),
             dma((3,)), dma((3,)),
             dma((16,)), dma((EXPERTS,)),
         ],
         compiler_params=pltpu.CompilerParams(
-            collective_id=0, has_side_effects=True, vmem_limit_bytes=48 * 1024 * 1024
+            collective_id=0, has_side_effects=True, vmem_limit_bytes=VMEM_LIMIT
         ),
         cost_estimate=pl.CostEstimate(flops=5 * 10**9, bytes_accessed=10**7, transcendentals=10**6),
     )(x_rows, dy_rows, w_flat, w_down, counts, assign)
+    shapes = tuple(jax.ShapeDtypeStruct(part.shape, part.dtype) for part in held)
+    grad_in, grad_out, grad_tokens = pl.pallas_call(
+        copy_kernel,
+        out_shape=shapes,
+        in_specs=[anywhere] * 3,
+        out_specs=(anywhere,) * 3,
+        scratch_shapes=[pltpu.VMEM(part.shape, part.dtype) for part in shapes] + [dma((3,)), dma((3,))],
+        compiler_params=pltpu.CompilerParams(vmem_limit_bytes=VMEM_LIMIT),
+    )(*held)
     grad_w_in = jnp.transpose(grad_in.reshape(2, units, quarter), (2, 0, 1))[None]
     grad_w_out = jnp.transpose(grad_out, (1, 0))[None]
     return grad_w_in, grad_w_out, grad_tokens

time: 100 us -> 82.9 us (0.83)
  Pallas kernels: 91.7 us -> 82 us
  local copies, waits for them, and re-layouts: 7.52 us -> 0 us
    pallas_call x1, Pallas kernels: 91.7 us -> 79.6 us  [per_device(): pl.pallas_call(fused_kernel, out_shape=(jax.ShapeDtypeStruct((2 * units,...]
    unnamed x13 -> x0, local copies, waits for them, and re-layouts: 7.52 us -> none
    pallas_call x0 -> x1, Pallas kernels: none -> 2.4 us  [per_device(): pl.pallas_call(copy_kernel, out_shape=shapes, in_specs=[anywhere] * 3, ou...]
where the time goes in v2:
time: 82.9 us; the launch traced here: 82.6 us
  Pallas kernels  82 us (99%)
    pallas_call x1, Pallas kernels, per_device(): pl.pallas_call(fused_kernel, out_shape=(jax.ShapeDtypeStruct((2 * units,...  79.6 us
    pallas_call x1, Pallas kernels, per_device(): pl.pallas_call(copy_kernel, out_shape=shapes, in_specs=[anywhere] * 3, ou...  2.4 us

profile of v2, /device:TPU:1, one launch (start us, length us, event | category | flops | bytes accessed | tf_op | source)
XLA Modules:
  0.0 82.6 jit_solution(428082130989039599)
XLA Ops:
  0.6 79.6 %shard_map.85 = (bf16[672,768]{1,0:T(8,128)(2,1)}, bf16[336,768]{1,0:T(8,128)(2,1)}, bf16[4,768]{1,0:T(4,128)(2,1)}) custom-call(bf16[128,3072]{1,0:T(8,128)(2,1)} %x_ref.1, bf16[128,3072]{1,0:T(8,128)(2,1)} %dy_ref.1, bf16[672,3072]{1,0:T(8,128)(2,1)} %bitcast.16, bf16[336,3072]{1,0:T(8,128)(2,1)} %bitcast.17, s32[1,64]{1,0:T(1,128)} %counts_ref.1, ...), custom_call_target="tpu_custom_call" | custom-call | flops 5000000000 | bytes 10000000 | tf_op jit(solution)/shard_map/pallas_call | solution.py:422
  80.2 2.4 %shard_map.86 = (bf16[672,768]{1,0:T(8,128)(2,1)}, bf16[336,768]{1,0:T(8,128)(2,1)}, bf16[4,768]{1,0:T(4,128)(2,1)}) custom-call(bf16[672,768]{1,0:T(8,128)(2,1)} %get-tuple-element.9.a_in, bf16[336,768]{1,0:T(8,128)(2,1)} %get-tuple-element.10.b_in, bf16[4,768]{1,0:T(4,128)(2,1)} %get-tuple-element.11.c_in), custom_call_target="tpu_custom_call" | custom-call | tf_op jit(solution)/shard_map/pallas_call | solution.py:462

commit v3 on v2

--- a/solution.py
+++ b/solution.py
@@ -12,7 +12,7 @@
 EXPERTS = 16
 SLOTS = 128
 QUARTERS = 4
-VMEM_LIMIT = 56 * 1024 * 1024
+VMEM_LIMIT = 54 * 1024 * 1024
 
 ROUNDS = (
     ((3, 0), (1, 3)),
@@ -127,17 +127,17 @@
         block = at(core, d, q, start, 16)
         return rcopy(block, block, xs.at[i], xr.at[i], {"expert": u + flip_x})
 
-    def y_copy(i, way, block_m):
+    def y_copy(i, way, block_m, side):
         d, q = CHUNKS[i]
-        block = at(core, d, q, block_m * 32, 32)
-        j = 4 * i + way
-        return rcopy(block, block, ys.at[j], yr.at[j], {"mp": m_at[1] if way == 0 else m_at[3]})
+        block = at(core, d, q, block_m * 32 + 16 * side, 16)
+        j = 2 * way + side
+        return rcopy(block, block, ys.at[i, j], yr.at[i, j], {"mp": m_at[1] if way == 0 else m_at[3]})
 
     def y_forward(i, way, block_m):
         d, q = CHUNKS[i]
         block = at(core, d, q, block_m * 32 + 16 * way, 16)
-        j = 4 * i + 2 + way
-        return rcopy(block, block, ys.at[j], yr.at[j], {"mp": m_at[1] if way == 0 else m_at[3]})
+        j = 4 + way
+        return rcopy(block, block, ys.at[i, j], yr.at[i, j], {"mp": m_at[1] if way == 0 else m_at[3]})
 
     def c_copy(i, kind):
         d, q = CHUNKS[i]
@@ -153,18 +153,22 @@
             if k + WINDOW < len(ROUNDS):
                 z_copy(i + 2 * WINDOW).start()
             x_copy(i, own_16).start()
+            for way in range(2):
+                y_copy(i, way, m, half_x).start()
 
     def stage_x(k):
         for i in (2 * k, 2 * k + 1):
             x_copy(i, pair_16).wait_recv()
             for way in range(2):
-                y_copy(i, way, m).start()
+                y_copy(i, way, m, 1 - half_x).start()
 
     def stage_y(k):
         for i in (2 * k, 2 * k + 1):
-            y_copy(i, 0, m_at[3]).wait_recv()
+            y_copy(i, 0, m_at[3], half_x).wait_recv()
+            y_copy(i, 0, m_at[3], 1 - half_x).wait_recv()
             y_forward(i, 0, m_at[3]).start()
-            y_copy(i, 1, m_at[1]).wait_recv()
+            y_copy(i, 1, m_at[1], half_x).wait_recv()
+            y_copy(i, 1, m_at[1], 1 - half_x).wait_recv()
             y_forward(i, 1, m_at[1]).start()
 
     def stage_f(k):
@@ -347,7 +351,8 @@
             z_copy(i).wait_send()
             x_copy(i, own_16).wait_send()
             for way in range(2):
-                y_copy(i, way, m).wait_send()
+                for side in range(2):
+                    y_copy(i, way, m, side).wait_send()
                 y_forward(i, way, m_at[3] if way == 0 else m_at[1]).wait_send()
             c_copy(i, core).wait_send()
 
@@ -396,9 +401,15 @@
 
 
 def copy_kernel(a_in, b_in, c_in, a_out, b_out, c_out, a_held, b_held, c_held, in_sem, out_sem):
-    held = (a_held, b_held, c_held)
-    reads = [pltpu.make_async_copy(src, held[i], in_sem.at[i]) for i, src in enumerate((a_in, b_in, c_in))]
-    writes = [pltpu.make_async_copy(held[i], dst, out_sem.at[i]) for i, dst in enumerate((a_out, b_out, c_out))]
+    pieces = []
+    for src, held, dst in ((a_in, a_held, a_out), (b_in, b_held, b_out)):
+        size = 112
+        for first in range(0, src.shape[0], size):
+            cut = pl.ds(first, size)
+            pieces.append((src.at[cut], held.at[cut], dst.at[cut]))
+    pieces.append((c_in, c_held, c_out))
+    reads = [pltpu.make_async_copy(src, held, in_sem.at[i]) for i, (src, held, _) in enumerate(pieces)]
+    writes = [pltpu.make_async_copy(held, dst, out_sem.at[i]) for i, (_, held, dst) in enumerate(pieces)]
     for copy in reads:
         copy.start()
     for read, write in zip(reads, writes):
@@ -447,7 +458,7 @@
             dma((18,)),
             dma((12,)), dma((12,)),
             dma((12,)), dma((12,)),
-            dma((48,)), dma((48,)),
+            dma((12, 6)), dma((12, 6)),
             dma((48,)), dma((48,)),
             dma((3,)), dma((3,)),
             dma((3,)), dma((3,)),
@@ -464,7 +475,7 @@
         out_shape=shapes,
         in_specs=[anywhere] * 3,
         out_specs=(anywhere,) * 3,
-        scratch_shapes=[pltpu.VMEM(part.shape, part.dtype) for part in shapes] + [dma((3,)), dma((3,))],
+        scratch_shapes=[pltpu.VMEM(part.shape, part.dtype) for part in shapes] + [dma((10,)), dma((10,))],
         compiler_params=pltpu.CompilerParams(vmem_limit_bytes=VMEM_LIMIT),
     )(*held)
     grad_w_in = jnp.transpose(grad_in.reshape(2, units, quarter), (2, 0, 1))[None]

time: 82.9 us -> 82.6 us (level)
  no operation moved by 1% of the time
where the time goes in v3:
time: 82.6 us; the launch traced here: 82.3 us
  Pallas kernels  81.7 us (99%)
    pallas_call x1, Pallas kernels, per_device(): pl.pallas_call(fused_kernel, out_shape=(jax.ShapeDtypeStruct((2 * units,...  79.3 us
    pallas_call x1, Pallas kernels, per_device(): pl.pallas_call(copy_kernel, out_shape=shapes, in_specs=[anywhere] * 3, ou...  2.33 us

profile of v3, /device:TPU:1, one launch (start us, length us, event | category | flops | bytes accessed | tf_op | source)
XLA Modules:
  0.0 82.3 jit_solution(8282731176094387486)
XLA Ops:
  0.6 79.3 %shard_map.85 = (bf16[672,768]{1,0:T(8,128)(2,1)}, bf16[336,768]{1,0:T(8,128)(2,1)}, bf16[4,768]{1,0:T(4,128)(2,1)}) custom-call(bf16[128,3072]{1,0:T(8,128)(2,1)} %x_ref.1, bf16[128,3072]{1,0:T(8,128)(2,1)} %dy_ref.1, bf16[672,3072]{1,0:T(8,128)(2,1)} %bitcast.16, bf16[336,3072]{1,0:T(8,128)(2,1)} %bitcast.17, s32[1,64]{1,0:T(1,128)} %counts_ref.1, ...), custom_call_target="tpu_custom_call" | custom-call | flops 5000000000 | bytes 10000000 | tf_op jit(solution)/shard_map/pallas_call | solution.py:433
  80.0 2.3 %shard_map.86 = (bf16[672,768]{1,0:T(8,128)(2,1)}, bf16[336,768]{1,0:T(8,128)(2,1)}, bf16[4,768]{1,0:T(4,128)(2,1)}) custom-call(bf16[672,768]{1,0:T(8,128)(2,1)} %get-tuple-element.9.a_in, bf16[336,768]{1,0:T(8,128)(2,1)} %get-tuple-element.10.b_in, bf16[4,768]{1,0:T(4,128)(2,1)} %get-tuple-element.11.c_in), custom_call_target="tpu_custom_call" | custom-call | tf_op jit(solution)/shard_map/pallas_call | solution.py:473
